TPU v7x, 32 devices: a whole 2x2x4 slice. The times are simulated.
32 devices in a mesh: groups: 2 (over x), lon: 16 (over z, y, core).
Axes of the slice: x: 2, y: 2, z: 4, core: 2. Of those that a mesh axis runs over, the one named last changes fastest.
Arguments:
- queries: bfloat16 [8192, 1024], P(('groups', 'lon')), parts along dimension 0, may hold values from -8 to 8
- key_tokens: bfloat16 [8192, 1024], P(('groups', 'lon')), parts along dimension 0, may hold values from -8 to 8
- value_tokens: bfloat16 [8192, 1024], P(('groups', 'lon')), parts along dimension 0, may hold values from -6 to 6
- grad_out: bfloat16 [8192, 1024], P(('groups', 'lon')), parts along dimension 0, may hold values from -6 to 6
- out_weight: bfloat16 [1024, 1024], replicated, may hold values from -3 to 3
- pattern: int32 [32, 3], replicated, may hold values from 0 to 31, as said below
- valid_rows: int32 [32], replicated, may hold values from 64 to 128, as said below
Outputs:
- layer_out: bfloat16 [8192, 1024], P(('groups', 'lon')), parts along dimension 0
- grad_queries: bfloat16 [8192, 1024], P(('groups', 'lon')), parts along dimension 0
- grad_keys: bfloat16 [8192, 1024], P(('groups', 'lon')), parts along dimension 0
- grad_values: bfloat16 [8192, 1024], P(('groups', 'lon')), parts along dimension 0
There are 2 independent parts, one for each index of `groups`. A program takes and returns all parts, laid end to end along the dimension named above; an argument that names none is the same for every part. Nothing has to cross between parts.
Inputs may be any that keep to these rules, and one draw needn't show every extreme that they name: `pattern`: block g lies in longitude strip g // 2 at latitude index g % 2. Row g names three key blocks: column 1 is g itself, column 0 a block of strip (g // 2 - 1) mod 16, column 2 a block of strip (g // 2 + 1) mod 16, each at a latitude index that differs from g's by at most one. The first valid_rows[g] tokens of block g are live, the others are padding.
All inputs are finite; a program needn't handle non-finite values.
Results may differ from a plain program's by a relative error of at most 0.028.
Values may be sent and summed in bfloat16 or wider, within the bound.
A program may use at most 128 MiB of HBM per device.

v0:
```python
import jax
import jax.numpy as jnp
from jax import lax
from jax.sharding import PartitionSpec as P

HEADS = 16
TILE = 128


def with_halo(cells, sides, width):
    for axis, dim in sides:
        count = lax.axis_size(axis)
        head = lax.slice_in_dim(cells, 0, width, axis=dim)
        tail = lax.slice_in_dim(cells, cells.shape[dim] - width, cells.shape[dim], axis=dim)
        cells = jnp.concatenate(
            [
                lax.ppermute(tail, axis, [(i, (i + 1) % count) for i in range(count)]),
                cells,
                lax.ppermute(head, axis, [((i + 1) % count, i) for i in range(count)]),
            ],
            axis=dim,
        )
    return cells


def passed_along(block, axis, distance):
    devices = range(lax.axis_size(axis))
    route = [((i - distance) % len(devices), i) for i in devices]
    return lax.ppermute(block, axis, route)


def split_heads(tensor):
    return tensor.reshape(tensor.shape[:-1] + (HEADS, tensor.shape[-1] // HEADS))


def live_rows(counts):
    return jnp.arange(TILE, dtype=jnp.int32)[None, :] < counts[:, None]


def per_device(queries, key_tokens, value_tokens, grad_out, out_weight, pattern, valid_rows):
    strip_count = lax.axis_size("lon")
    position = lax.axis_index("lon")
    row_count, features = queries.shape
    blocks = row_count // TILE
    score_scale = (features // HEADS) ** (-0.5)
    near_span = 3 * TILE
    strips = (position + jnp.arange(3, dtype=jnp.int32) - 1) % strip_count
    near_counts = jnp.stack(
        [
            lax.dynamic_slice_in_dim(valid_rows, strips[offset] * blocks, blocks, 0)
            for offset in range(3)
        ]
    )
    near_pattern = jnp.stack(
        [
            lax.dynamic_slice_in_dim(pattern, strips[offset] * blocks, blocks, 0)
            for offset in range(3)
        ]
    )
    near_live = live_rows(near_counts.reshape(-1)).reshape(3, blocks, TILE)
    own_live = near_live[1]
    root_counts = jnp.sqrt(near_counts[1].astype(jnp.float32))
    picked = jnp.arange(3, dtype=jnp.int32)[None, :] * blocks + near_pattern[1] % blocks
    key_value = jnp.stack((key_tokens, value_tokens))
    bordered = with_halo(key_value, (("lon", 1),), row_count)
    bordered = bordered.reshape(2, 3 * blocks, TILE, features)
    pooled = jnp.einsum(
        "gt,xgtd->xgd",
        own_live.astype(jnp.bfloat16),
        key_value.reshape(2, blocks, TILE, features),
        preferred_element_type=jnp.float32,
    )
    summary = (pooled / root_counts[None, :, None]).astype(jnp.bfloat16)
    summaries = lax.all_gather(summary, "lon", axis=1, tiled=True)
    far_keys = split_heads(summaries[0])
    far_values = split_heads(summaries[1])
    far_count = summaries.shape[1]
    near_pairs = bordered[:, picked].reshape(2, blocks, near_span, features)
    near_keys = split_heads(near_pairs[0])
    near_values = split_heads(near_pairs[1])
    near_mask = near_live.reshape(3 * blocks, TILE)[picked].reshape(blocks, near_span)
    query_heads = split_heads(queries.reshape(blocks, TILE, features))
    near_scores = (
        jnp.einsum("bthc,blhc->bhtl", query_heads, near_keys, preferred_element_type=jnp.float32)
        * score_scale
    )
    near_scores = jnp.where(near_mask[:, None, None, :], near_scores, -jnp.inf)
    far_scores = (
        jnp.einsum("bthc,shc->bhts", query_heads, far_keys, preferred_element_type=jnp.float32)
        * score_scale
    )
    row_top = jnp.maximum(jnp.max(near_scores, axis=-1), jnp.max(far_scores, axis=-1))
    total = jnp.sum(jnp.exp(near_scores - row_top[..., None]), axis=-1) + jnp.sum(
        jnp.exp(far_scores - row_top[..., None]), axis=-1
    )
    log_total = row_top + jnp.log(total)
    near_chances = jnp.exp(near_scores - log_total[..., None])
    far_chances = jnp.exp(far_scores - log_total[..., None])
    near_rounded = near_chances.astype(jnp.bfloat16)
    far_rounded = far_chances.astype(jnp.bfloat16)
    mixed_heads = jnp.einsum(
        "bhtl,blhc->bthc", near_rounded, near_values, preferred_element_type=jnp.float32
    )
    mixed_heads = mixed_heads + jnp.einsum(
        "bhts,shc->bthc", far_rounded, far_values, preferred_element_type=jnp.float32
    )
    attended = mixed_heads.astype(jnp.bfloat16)
    layer_out = jnp.dot(
        attended.reshape(row_count, features), out_weight, preferred_element_type=jnp.float32
    ).astype(jnp.bfloat16)
    grad_attended = lax.dot_general(
        grad_out, out_weight, (((1,), (1,)), ((), ())), preferred_element_type=jnp.float32
    ).astype(jnp.bfloat16)
    grad_heads = split_heads(grad_attended.reshape(blocks, TILE, features))
    row_delta = jnp.einsum(
        "bthc,bthc->bht", grad_heads, attended, preferred_element_type=jnp.float32
    )
    near_grad_chances = jnp.einsum(
        "bthc,blhc->bhtl", grad_heads, near_values, preferred_element_type=jnp.float32
    )
    far_grad_chances = jnp.einsum(
        "bthc,shc->bhts", grad_heads, far_values, preferred_element_type=jnp.float32
    )
    near_grad_scores = (
        near_chances * (near_grad_chances - row_delta[..., None]) * score_scale
    ).astype(jnp.bfloat16)
    far_grad_scores = (
        far_chances * (far_grad_chances - row_delta[..., None]) * score_scale
    ).astype(jnp.bfloat16)
    grad_query = jnp.einsum(
        "bhtl,blhc->bthc", near_grad_scores, near_keys, preferred_element_type=jnp.float32
    )
    grad_query = grad_query + jnp.einsum(
        "bhts,shc->bthc", far_grad_scores, far_keys, preferred_element_type=jnp.float32
    )
    grad_queries = grad_query.astype(jnp.bfloat16).reshape(row_count, features)
    far_grad_keys = jnp.einsum(
        "bhts,bthc->shc", far_grad_scores, query_heads, preferred_element_type=jnp.float32
    ).reshape(far_count, features)
    far_grad_values = jnp.einsum(
        "bhts,bthc->shc", far_rounded, grad_heads, preferred_element_type=jnp.float32
    ).reshape(far_count, features)
    far_grads = lax.psum_scatter(
        jnp.stack((far_grad_keys, far_grad_values)), "lon", scatter_dimension=1, tiled=True
    )
    spread = (
        own_live.astype(jnp.float32)[None, :, :, None]
        * (far_grads / root_counts[None, :, None])[:, :, None, :]
    )
    spread = spread.reshape(2, row_count, features)
    near_grad_keys = jnp.einsum(
        "bhtl,bthc->blhc", near_grad_scores, query_heads, preferred_element_type=jnp.float32
    )
    near_grad_values = jnp.einsum(
        "bhtl,bthc->blhc", near_rounded, grad_heads, preferred_element_type=jnp.float32
    )
    onehot = (
        picked.reshape(-1)[:, None] == jnp.arange(3 * blocks, dtype=jnp.int32)[None, :]
    ).astype(jnp.float32)
    stacked = jnp.stack((near_grad_keys, near_grad_values)).reshape(2, 3 * blocks, TILE * features)
    placed = jnp.einsum("ne,xnk->xek", onehot, stacked, precision=lax.Precision.HIGHEST).reshape(
        2, 3, row_count, features
    )
    from_east = passed_along(placed[:, 0].astype(jnp.bfloat16), "lon", -1).astype(jnp.float32)
    from_west = passed_along(placed[:, 2].astype(jnp.bfloat16), "lon", 1).astype(jnp.float32)
    gathered = placed[:, 1] + from_east + from_west
    totals = gathered + spread
    return (layer_out, grad_queries, totals[0].astype(jnp.bfloat16), totals[1].astype(jnp.bfloat16))


def solution(mesh):
    return jax.shard_map(
        per_device,
        mesh=mesh,
        in_specs=(
            P(("groups", "lon"), None),
            P(("groups", "lon"), None),
            P(("groups", "lon"), None),
            P(("groups", "lon"), None),
            P(),
            P(),
            P(),
        ),
        out_specs=(
            P(("groups", "lon"), None),
            P(("groups", "lon"), None),
            P(("groups", "lon"), None),
            P(("groups", "lon"), None),
        ),
        check_vma=False,
    )
```

profile of v0, /device:TPU:0, one launch (start us, length us, event | category | flops | bytes accessed | tf_op | source)
XLA Modules:
  0.0 214.0 jit_solution(10437834198670715514)
XLA Ops:
  7.2 2.4 %pad_maximum_fusion.1 = bf16[2,256,1024]{2,1,0:T(8,128)(2,1)} fusion(bf16[1,256,1024]{2,1,0:T(8,128)(2,1)} %bitcast.169, bf16[1,256,1024]{2,1,0:T(8,128)(2,1)} %bitcast.172), kind=kLoop, calls=%fused_computation.45 | loop fusion | flops 524288 | bytes 2097152 | tf_op jit(solution)/shard_map/stack | solution.py:64
  9.7 5.4 %collective-permute-start.1 = (bf16[2,256,1024]{2,1,0:T(8,128)(2,1)}, bf16[2,256,1024]{2,1,0:T(8,128)(2,1)}, u32[]{:S(2)}, u32[]{:S(2)}) collective-permute-start(bf16[2,256,1024]{2,1,0:T(8,128)(2,1)} %pad_maximum_fusion.1), channel_id=1, source_target_pairs={{1,0},{2,1},{3,2},{4,3},{5,4},{6,5},{7,6},{8,7},{9,8},{10,9},{11,1... | collective-permute-start | bytes 3145736 | tf_op jit(solution)/shard_map/ppermute | solution.py:19
  23.8 25.8 %all_gather.3 = bf16[2,32,1024]{2,0,1:T(2,128)(2,1)S(1)} all-gather(bf16[2,2,1024]{2,0,1:T(2,128)(2,1)S(1)} %fusion.47), channel_id=1, replica_groups=mesh['groups'=2,'lon'=16] {'lon'}, dimensions={1}, use_global_device_ids=true | all-gather | bytes 139264 | tf_op jit(solution)/shard_map/all_gather | solution.py:74
  50.8 2.6 %convolution_convert_fusion = bf16[256,1024]{1,0:T(8,128)(2,1)} fusion(bf16[256,1024]{1,0:T(8,128)(2,1)} %param.10, bf16[1024,1024]{1,0:T(8,128)(2,1)S(1)} %copy-done), kind=kOutput, calls=%fused_computation.30 | convolution fusion | flops 537133056 | bytes 3145728 | tf_op jit(solution)/shard_map/dot_general | solution.py:111
  57.0 2.4 %bitcast_convert_fusion = f32[2,16,128,64]{2,0,3,1:T(2,128)} fusion(bf16[2,128,16,64]{1,0,3,2:T(2,128)(2,1)} %reshape_reshape.7), kind=kLoop, calls=%fused_computation.54 | loop fusion | flops 262144 | bytes 1572864
  59.5 3.4 %pad_maximum_fusion = bf16[2,768,1024]{2,1,0:T(8,128)(2,1)} fusion(bf16[2,256,1024]{2,1,0:T(8,128)(2,1)} %collective-permute-done.1, bf16[1,256,1024]{2,1,0:T(8,128)(2,1)} %bitcast.171, bf16[1,256,1024]{2,1,0:T(8,128)(2,1)} %bitcast.174, bf16[2,256,1024]{2,1,0:T(8,128)(2,1)} %collective-permute-done), kind=kLoop, calls=%fused_computation.15 | loop fusion | flops 12582912 | bytes 6291456 | tf_op jit(solution)/shard_map/concatenate | solution.py:15
  62.9 4.4 %gather_fusion = bf16[6,2,128,1024]{3,2,1,0:T(8,128)(2,1)} fusion(bf16[2,6,128,1024]{3,2,1,0:T(8,128)(2,1)} %bitcast.168, s32[1024]{0:T(1024)S(1)} %pad_clamp_fusion), kind=kCustom, calls=%fused_computation | custom fusion | bytes 6291480 | tf_op jit(solution)/shard_map/gather | solution.py:78
  67.3 3.8 %fusion.62 = (bf16[1,2,3,128,1024]{4,3,0,2,1:T(8,128)(2,1)}, bf16[1,2,3,128,1024]{4,3,0,2,1:T(8,128)(2,1)}) fusion(bf16[2,2,3,128,1024]{4,3,0,2,1:T(8,128)(2,1)} %bitcast.167), kind=kLoop, calls=%fused_computation.116 | loop fusion | bytes 6291456 | tf_op jit(solution)/shard_map/slice | solution.py:80
  71.1 4.2 %copy.108 = bf16[1,2,3,128,1024]{3,2,4,1,0:T(4,128)(2,1)} copy(bf16[1,2,3,128,1024]{4,3,0,2,1:T(8,128)(2,1)} %get-tuple-element.22) | data formatting | bytes 3145728 | tf_op jit(solution)/shard_map/slice | solution.py:80
  75.3 5.1 %reshape_squeeze.12 = bf16[2,384,16,64]{1,3,2,0:T(8,128)(2,1)} reshape(bf16[1,2,3,128,1024]{3,2,4,1,0:T(4,128)(2,1)} %copy.108) | data formatting | bytes 3145728 | tf_op jit(solution)/shard_map/reshape;squeeze | solution.py:33
  80.4 4.2 %copy.109 = bf16[1,2,3,128,1024]{3,2,4,1,0:T(4,128)(2,1)} copy(bf16[1,2,3,128,1024]{4,3,0,2,1:T(8,128)(2,1)} %get-tuple-element.23) | data formatting | bytes 3145728 | tf_op jit(solution)/shard_map/slice | solution.py:79
  84.6 5.1 %reshape_squeeze.13 = bf16[2,384,16,64]{1,3,2,0:T(8,128)(2,1)} reshape(bf16[1,2,3,128,1024]{3,2,4,1,0:T(4,128)(2,1)} %copy.109) | data formatting | bytes 3145728 | tf_op jit(solution)/shard_map/reshape;squeeze | solution.py:33
  89.7 3.0 %bitcast_reduce_fusion = (f32[2,16,128]{2,1,0:T(8,128)S(1)}, f32[2,16,384,128]{3,2,1,0:T(8,128)S(1)}) fusion(pred[2,384]{1,0:T(4,128)(4,1)S(1)} %broadcast_in_dim.17, bf16[2,384,16,64]{1,3,2,0:T(8,128)(2,1)} %reshape_squeeze.13, bf16[2,128,16,64]{1,0,3,2:T(2,128)(2,1)S(1)} %reshape_reshape.6), kind=kOutput, calls=%fused_computation.8 | convolution fusion | flops 206041088 | bytes 8405760 | tf_op jit(solution)/shard_map/bthc,blhc->bhtl/dot_general | solution.py:84
  95.9 2.6 %multiply_reduce_fusion = (f32[2,16,128]{2,1,0:T(8,128)S(1)}, bf16[2,128,16,64]{1,3,2,0:T(8,128)(2,1)}) fusion(f32[2,16,128,64]{2,0,3,1:T(2,128)S(1)} %copy-done.7, f32[2,128,16,64]{1,3,2,0:T(8,128)S(1)} %convolution_bitcast_fusion.4, bf16[2,384,16,64]{1,3,2,0:T(8,128)(2,1)S(1)} %copy-done.5, f32[2,16,384,128]{3,2,1,0:T(8,128)S(1)} %get-tuple-element.35, ...), kind=kOutput, calls=%fused_computation.47 | convolution fusion | flops 208924672 | bytes 10519296 | tf_op jit(solution)/shard_map/bhtl,blhc->bthc/dot_general | solution.py:101
  99.1 3.9 %multiply_convert_fusion = bf16[2,16,128,384]{2,3,1,0:T(8,128)(2,1)} fusion(f32[2,16,384,128]{3,2,1,0:T(8,128)S(1)} %get-tuple-element.35, f32[2,16,128]{2,1,0:T(8,128)S(1)} %get-tuple-element.38, f32[2,16,128]{2,1,0:T(8,128)S(1)} %fusion.45, pred[2,384]{1,0:T(4,128)(4,1)S(1)} %broadcast_in_dim.17, bf16[2,384,16,64]{1,3,2,0:T(8,128)(2,1)S(1)} %copy-done.5, ...), kind=kOutput, calls=%fused_computation.12 | convolution fusion | flops 212336640 | bytes 11567872 | tf_op jit(solution)/shard_map/bthc,blhc->bhtl/dot_general | solution.py:118
  103.0 3.2 %convolution_bitcast_fusion.1 = f32[2,384,16,64]{1,3,2,0:T(8,128)} fusion(bf16[2,128,16,64]{1,0,3,2:T(2,128)(2,1)S(1)} %copy-done.2, f32[2,16,384,128]{3,2,1,0:T(8,128)S(1)} %get-tuple-element.35, f32[2,16,128]{2,1,0:T(8,128)S(1)} %fusion.45, pred[2,384]{1,0:T(4,128)(4,1)S(1)} %broadcast_in_dim.17), kind=kOutput, calls=%fused_computation.22 | convolution fusion | flops 207618048 | bytes 9978624 | tf_op jit(solution)/shard_map/bhtl,bthc->blhc/dot_general | solution.py:154
  107.2 2.4 %copy.121 = bf16[2,128,16,64]{1,0,3,2:T(2,128)(2,1)} copy(bf16[2,128,16,64]{1,3,2,0:T(8,128)(2,1)} %get-tuple-element.39) | data formatting | bytes 1048576 | tf_op jit(solution)/shard_map/convert_element_type | solution.py:107
  111.4 1.6 pad_maximum_fusion.3
  113.1 5.1 %convolution_bitcast_fusion.2 = f32[2,384,16,64]{1,3,2,0:T(8,128)} fusion(bf16[2,16,128,384]{2,3,1,0:T(8,128)(2,1)} %multiply_convert_fusion, bf16[2,128,16,64]{1,0,3,2:T(2,128)(2,1)S(1)} %reshape_reshape.6), kind=kOutput, calls=%fused_computation.23 | convolution fusion | flops 201326592 | bytes 6815744 | tf_op jit(solution)/shard_map/bhtl,bthc->blhc/dot_general | solution.py:151
  118.2 6.1 %copy.134 = f32[2,384,16,64]{3,2,1,0:T(8,128)} copy(f32[2,384,16,64]{1,3,2,0:T(8,128)} %convolution_bitcast_fusion.2) | data formatting | bytes 6291456 | tf_op jit(solution)/shard_map/bhtl,bthc->blhc/transpose | solution.py:151
  124.3 6.6 %stack.49 = f32[1,6,131072]{2,1,0:T(8,128)} reshape(f32[2,384,16,64]{3,2,1,0:T(8,128)} %copy.134) | data formatting | bytes 6291456 | tf_op jit(solution)/shard_map/stack | solution.py:160
  130.9 6.1 %copy.137 = f32[2,384,16,64]{3,2,1,0:T(8,128)} copy(f32[2,384,16,64]{1,3,2,0:T(8,128)} %convolution_bitcast_fusion.1) | data formatting | bytes 6291456 | tf_op jit(solution)/shard_map/bhtl,bthc->blhc/transpose | solution.py:154
  137.0 6.6 %stack.50 = f32[1,6,131072]{2,1,0:T(8,128)} reshape(f32[2,384,16,64]{3,2,1,0:T(8,128)} %copy.137) | data formatting | bytes 6291456 | tf_op jit(solution)/shard_map/stack | solution.py:160
  143.7 11.1 %convolution_bitcast_fusion = f32[2,6,131072]{2,1,0:T(8,128)} fusion(f32[1,6,131072]{2,1,0:T(8,128)} %stack.50, f32[1,6,131072]{2,1,0:T(8,128)} %stack.49, s32[6]{0:T(128)S(1)} %copy-done.12), kind=kOutput, calls=%fused_computation.2 | convolution fusion | flops 114819104 | bytes 12582936 | tf_op jit(solution)/shard_map/ne,xnk->xek/dot_general | solution.py:161
  154.8 7.2 %reshape.84 = f32[2,3,256,1024]{3,2,1,0:T(8,128)} reshape(f32[2,6,131072]{2,1,0:T(8,128)} %convolution_bitcast_fusion) | data formatting | bytes 12582912 | tf_op jit(solution)/shard_map/reshape | solution.py:161
  161.9 3.3 %convert.9 = bf16[2,3,256,1024]{3,2,1,0:T(8,128)(2,1)S(1)} convert(f32[2,3,256,1024]{3,2,1,0:T(8,128)} %reshape.84) | non-fusion elementwise | flops 1572864 | bytes 9437184 | tf_op jit(solution)/shard_map/convert.4
  165.2 1.5 slice_bitcast_fusion.2
  168.5 1.5 fusion.14
  170.1 1.5 convolution_convert_fusion.1
  171.6 1.8 copy.168
  175.0 27.4 %all-reduce.3.cloned.1.call-done = f32[2,32,1024]{2,1,0:T(8,128)} async-done(((f32[2,32,1024]{2,1,0:T(8,128)}), f32[2,32,1024]{2,1,0:T(8,128)}) %all-reduce.3.cloned.1.call-update) | async-done | bytes 262160
  203.3 2.8 %fusion.10 = bf16[2,256,1024]{2,1,0:T(8,128)(2,1)S(1)} fusion(f32[2,3,256,1024]{3,2,1,0:T(8,128)} %reshape.84, bf16[2,256,1024]{2,1,0:T(8,128)(2,1)} %collective-permute-done.3, bf16[2,256,1024]{2,1,0:T(8,128)(2,1)} %collective-permute-done.2, f32[2,2,1024]{2,1,0:T(2,128)S(1)} %dynamic-slice_divide_fusion, f32[256]{0:T(256)S(1)} %copy-done.9), kind=kLoop, calls=%fused_computation.20 | loop fusion | flops 3670016 | bytes 5260288 | tf_op jit(solution)/shard_map/convert.2
  (84 shorter events, 22.7 us)
Async XLA Ops:
  7.2 43.6 %copy-start = (bf16[1024,1024]{1,0:T(8,128)(2,1)S(1)}, bf16[1024,1024]{1,0:T(8,128)(2,1)}, u32[]{:S(2)}) copy-start(bf16[1024,1024]{1,0:T(8,128)(2,1)} %param.11) | copy-start | bytes 6291460
  7.2 43.3 %copy-start.8 = (bf16[256,1024]{1,0:T(8,128)(2,1)S(1)}, bf16[256,1024]{1,0:T(8,128)(2,1)}, u32[]{:S(2)}) copy-start(bf16[256,1024]{1,0:T(8,128)(2,1)} %param.7) | copy-start | bytes 1572868
  7.2 195.2 %all-reduce.3.cloned.1.call-start = ((), (), s32[]{:S(2)}) async-start(), calls=%async_computation | async-start | bytes 524288
  9.7 49.8 %collective-permute-start.1 = (bf16[2,256,1024]{2,1,0:T(8,128)(2,1)}, bf16[2,256,1024]{2,1,0:T(8,128)(2,1)}, u32[]{:S(2)}, u32[]{:S(2)}) collective-permute-start(bf16[2,256,1024]{2,1,0:T(8,128)(2,1)} %pad_maximum_fusion.1), channel_id=1, source_target_pairs={{1,0},{2,1},{3,2},{4,3},{5,4},{6,5},{7,6},{8,7},{9,8},{10,9},{11,1... | collective-permute-start | bytes 3145736 | tf_op jit(solution)/shard_map/ppermute | solution.py:19
  15.1 44.3 %collective-permute-start = (bf16[2,256,1024]{2,1,0:T(8,128)(2,1)}, bf16[2,256,1024]{2,1,0:T(8,128)(2,1)}, u32[]{:S(2)}, u32[]{:S(2)}) collective-permute-start(bf16[2,256,1024]{2,1,0:T(8,128)(2,1)} %pad_maximum_fusion.1), channel_id=1, source_target_pairs={{0,1},{1,2},{2,3},{3,4},{4,5},{5,6},{6,7},{7,8},{8,9},{9,10},{10,1... | collective-permute-start | bytes 3145736 | tf_op jit(solution)/shard_map/ppermute | solution.py:17
  18.4 5.4 %copy-start.10 = (f32[2]{0:T(128)}, f32[2]{0:T(128)S(1)}, u32[]{:S(2)}) copy-start(f32[2]{0:T(128)S(1)} %convert_sqrt_fusion) | copy-start | bytes 28
  50.3 44.4 %copy-start.6 = (bf16[32,16,64]{2,1,0:T(8,128)(2,1)}, bf16[32,16,64]{2,1,0:T(8,128)(2,1)S(1)}, u32[]{:S(2)}) copy-start(bf16[32,16,64]{2,1,0:T(8,128)(2,1)S(1)} %reshape_squeeze.15) | copy-start | bytes 196612
  50.6 4.9 %copy-start.13 = (u32[32]{0:T(128)S(1)}, u32[32]{0:T(128)}, u32[]{:S(2)}) copy-start(u32[32]{0:T(128)} %constant.57) | copy-start | bytes 388
  92.7 1.6 copy-start.2
  94.2 1.4 copy-start.5
  94.2 1.7 copy-start.7
  137.0 6.6 %copy-start.12 = (s32[6]{0:T(128)S(1)}, s32[6]{0:T(128)}, u32[]{:S(2)}) copy-start(s32[6]{0:T(128)} %eq.19) | copy-start | bytes 76
  165.2 3.3 %copy-start.1 = (bf16[2,384,16,64]{1,3,2,0:T(8,128)(2,1)S(1)}, bf16[2,384,16,64]{1,3,2,0:T(8,128)(2,1)}, u32[]{:S(2)}) copy-start(bf16[2,384,16,64]{1,3,2,0:T(8,128)(2,1)} %reshape_squeeze.13) | copy-start | bytes 4718596
  165.2 3.3 %copy-start.3 = (bf16[2,16,128,384]{2,3,1,0:T(8,128)(2,1)S(1)}, bf16[2,16,128,384]{2,3,1,0:T(8,128)(2,1)}, u32[]{:S(2)}) copy-start(bf16[2,16,128,384]{2,3,1,0:T(8,128)(2,1)} %multiply_convert_fusion) | copy-start | bytes 9437188
  166.7 36.6 %collective-permute-start.2 = (bf16[2,256,1024]{2,1,0:T(8,128)(2,1)}, bf16[2,256,1024]{2,1,0:T(8,128)(2,1)}, u32[]{:S(2)}, u32[]{:S(2)}) collective-permute-start(bf16[2,256,1024]{2,1,0:T(8,128)(2,1)} %get-tuple-element.20), channel_id=1, source_target_pairs={{1,0},{2,1},{3,2},{4,3},{5,4},{6,5},{7,6},{8,7},{9,8},{10,9},{11,1... | collective-permute-start | bytes 3145736 | tf_op jit(solution)/shard_map/ppermute | solution.py:29
  168.2 35.1 %collective-permute-start.3 = (bf16[2,256,1024]{2,1,0:T(8,128)(2,1)}, bf16[2,256,1024]{2,1,0:T(8,128)(2,1)}, u32[]{:S(2)}, u32[]{:S(2)}) collective-permute-start(bf16[2,256,1024]{2,1,0:T(8,128)(2,1)} %get-tuple-element.21), channel_id=1, source_target_pairs={{15,0},{0,1},{1,2},{2,3},{3,4},{4,5},{5,6},{6,7},{7,8},{8,9},{9,10... | collective-permute-start | bytes 3145736 | tf_op jit(solution)/shard_map/ppermute | solution.py:29
  168.5 1.6 copy-start.4
  170.1 32.3 %copy-start.11 = (f32[2]{0:T(128)S(1)}, f32[2]{0:T(128)}, u32[]{:S(2)}) copy-start(f32[2]{0:T(128)} %copy-done.10) | copy-start | bytes 28
  170.1 33.2 %copy-start.9 = (f32[256]{0:T(256)S(1)}, f32[256]{0:T(256)}, u32[]{:S(2)}) copy-start(f32[256]{0:T(256)} %get-tuple-element.26) | copy-start | bytes 3076
Sparse Core Ops, SparseCore 0:
  113.2 89.1 all-reduce.2
where the time goes:
time: 215 us; the launch traced here: 214 us
  local copies, waits for them, and re-layouts  77.4 us (36%)
  matrix products  38.8 us (18%)
  waiting for transfers between devices  27.4 us (13%)
  blocking collectives  25.8 us (12%)
  other arithmetic  20.7 us (10%)
  between operations  16.9 us (8%)
  starting transfers between devices  6.92 us (3%)
    unnamed x2, waiting for transfers between devices  27.4 us
    all_gather x1, blocking collectives, per_device(): summaries = lax.all_gather(summary, 'lon', axis=1, tiled=True)  25.8 us
    another operation x2, local copies, waits for them, and re-layouts, per_device(): jnp.stack((near_grad_keys, near_grad_values))  13.3 us
    another operation x6, local copies, waits for them, and re-layouts, split_heads(): tensor.reshape(tensor.shape[:-1] + (HEADS, tensor.shape[-1] // HEADS))  11.6 us
    dot_general x1, matrix products, per_device(): jnp.einsum('ne,xnk->xek', onehot, stacked, precision=lax.Precision.HIGHEST)  11.1 us
    slice x2, local copies, waits for them, and re-layouts, per_device(): near_values = split_heads(near_pairs[1])  7.98 us
    reshape x1, local copies, waits for them, and re-layouts, per_device(): jnp.einsum('ne,xnk->xek', onehot, stacked, precision=lax.Precision.HIGHEST)  7.16 us
    transpose x1, local copies, waits for them, and re-layouts, per_device(): jnp.einsum('bhtl,bthc->blhc', near_grad_scores, query_heads, preferred_el...  6.11 us
  transfers between devices with their start and end apart: 5, of which 1 were waited for; matrix products, arithmetic and copies ran while one was open for 36% of the time, Pallas kernels for 0%

commit v1 on v0

v1 whole, which is shorter than its diff:
```python
import functools

import jax
import jax.numpy as jnp
from jax import lax
from jax.experimental import pallas as pl
from jax.experimental.pallas import tpu as pltpu
from jax.sharding import PartitionSpec as P

HEADS = 16
TILE = 128
PAIR = 128
GROUP = 256
AHEAD = 2
F32 = jnp.float32
BF16 = jnp.bfloat16


def nn(a, b):
    return lax.dot_general(a, b, (((1,), (0,)), ((), ())), preferred_element_type=F32)


def nt(a, b):
    return lax.dot_general(a, b, (((1,), (1,)), ((), ())), preferred_element_type=F32)


def tn(a, b):
    return lax.dot_general(a, b, (((0,), (0,)), ((), ())), preferred_element_type=F32)


def kernel(
    count,
    pattern, valid, queries, keys, values, grad_out, weight,
    layer_out, grad_queries, grad_keys, grad_values,
    halo, back_out, back_in, own, attended, grad_att,
    gathered, far_kv, far_sum, far_out, far_in,
    halo_send, halo_recv, back_send, back_recv,
    sum_send, sum_recv, far_send, far_recv,
):
    me = lax.axis_index("lon")
    east = lax.rem(me + 1, count)
    west = lax.rem(me + count - 1, count)
    rows, features = queries.shape
    pairs = features // PAIR
    groups = features // GROUP
    n_blocks = 2 * count
    kv_refs = (keys, values)
    sides = (west, east)

    def peer(step):
        return lax.rem(me + step, count)

    def source(step):
        return lax.rem(me + count - step, count)

    barrier = pltpu.get_barrier_semaphore()

    def greet(step, carry):
        pl.semaphore_signal(
            barrier, inc=1, device_id={"lon": peer(step)}, device_id_type=pl.DeviceIdType.MESH
        )
        return carry

    lax.fori_loop(1, count, greet, 0)
    pl.semaphore_wait(barrier, count - 1)

    def columns(pair):
        return pl.ds(pl.multiple_of(pair * PAIR, PAIR), PAIR)

    def halo_copy(side, kind, pair):
        return pltpu.make_async_remote_copy(
            src_ref=kv_refs[kind].at[:, columns(pair)],
            dst_ref=halo.at[1 - side, kind, :, columns(pair)],
            send_sem=halo_send.at[side, kind, pair],
            recv_sem=halo_recv.at[1 - side, kind, pair],
            device_id={"lon": sides[side]},
            device_id_type=pl.DeviceIdType.MESH,
        )

    def halo_arrival(slot, kind, pair):
        return pltpu.make_async_remote_copy(
            src_ref=kv_refs[kind].at[:, columns(pair)],
            dst_ref=halo.at[slot, kind, :, columns(pair)],
            send_sem=halo_send.at[slot, kind, pair],
            recv_sem=halo_recv.at[slot, kind, pair],
            device_id={"lon": sides[slot]},
            device_id_type=pl.DeviceIdType.MESH,
        )

    def back_copy(side, kind, pair):
        return pltpu.make_async_remote_copy(
            src_ref=back_out.at[side, kind, :, columns(pair)],
            dst_ref=back_in.at[1 - side, kind, :, columns(pair)],
            send_sem=back_send.at[side, kind, pair],
            recv_sem=back_recv.at[1 - side, kind, pair],
            device_id={"lon": sides[side]},
            device_id_type=pl.DeviceIdType.MESH,
        )

    def back_arrival(slot, kind, pair):
        return pltpu.make_async_remote_copy(
            src_ref=back_out.at[slot, kind, :, columns(pair)],
            dst_ref=back_in.at[slot, kind, :, columns(pair)],
            send_sem=back_send.at[slot, kind, pair],
            recv_sem=back_recv.at[slot, kind, pair],
            device_id={"lon": sides[slot]},
            device_id_type=pl.DeviceIdType.MESH,
        )

    def summary_copy(step, slot):
        return pltpu.make_async_remote_copy(
            src_ref=gathered.at[slot],
            dst_ref=gathered.at[slot],
            send_sem=sum_send.at[step],
            recv_sem=sum_recv.at[step],
            device_id={"lon": peer(step)},
            device_id_type=pl.DeviceIdType.MESH,
        )

    def far_copy(step, taken, slot):
        return pltpu.make_async_remote_copy(
            src_ref=far_out.at[taken],
            dst_ref=far_in.at[slot],
            send_sem=far_send.at[step],
            recv_sem=far_recv.at[step],
            device_id={"lon": peer(step)},
            device_id_type=pl.DeviceIdType.MESH,
        )

    def send_halo(pair):
        for kind in range(2):
            for side in range(2):
                halo_copy(side, kind, pair).start()

    send_halo(0)

    own_count = [valid[2 * me + b] for b in range(2)]
    root_row = lax.broadcasted_iota(jnp.int32, (16, GROUP), 0)
    root = jnp.sqrt(
        jnp.where(root_row % 2 == 0, own_count[0], own_count[1]).astype(F32)
    )
    pool_row = lax.broadcasted_iota(jnp.int32, (16, rows), 0)
    pool_col = lax.broadcasted_iota(jnp.int32, (16, rows), 1)
    pool_live = pool_col < jnp.where(pool_col < TILE, own_count[0], own_count[1] + TILE)
    pool_block = jnp.where(pool_col < TILE, 0, 1)
    pooled = jnp.zeros((16, GROUP), F32)
    for c in range(groups):
        for kind in range(2):
            chosen = (pool_row == 4 * c + 2 * kind + pool_block) & pool_live
            pooled += nn(
                chosen.astype(F32).astype(BF16), kv_refs[kind][:, c * GROUP : (c + 1) * GROUP]
            )
    gathered[me] = (pooled / root).astype(BF16)

    def send_summary(step, carry):
        summary_copy(step, me).start()
        return carry

    lax.fori_loop(1, count, send_summary, 0)
    for pair in range(1, AHEAD):
        send_halo(pair)

    for c in range(groups):
        part = slice(c * GROUP, (c + 1) * GROUP)
        grad_att[:, part] = nt(grad_out[...], weight[part, :]).astype(BF16)

    def take_summary(step, carry):
        summary_copy(step, source(step)).wait_recv()
        return carry

    lax.fori_loop(1, count, take_summary, 0)
    pieces = gathered[...].reshape(count * 16, GROUP)
    sel_row = lax.broadcasted_iota(jnp.int32, (n_blocks, count * 16), 0)
    sel_col = lax.broadcasted_iota(jnp.int32, (n_blocks, count * 16), 1)
    sel_place = (sel_row // 2) * 16 + sel_row % 2
    for c in range(groups):
        for kind in range(2):
            chosen = (sel_col == sel_place + (4 * c + 2 * kind)).astype(F32).astype(BF16)
            far_kv[kind, :, c * GROUP : (c + 1) * GROUP] = nn(chosen, pieces).astype(BF16)

    lane = lax.broadcasted_iota(jnp.int32, (1, PAIR), 1)
    first = (lane < PAIR // 2).astype(F32).astype(BF16)
    second = (lane >= PAIR // 2).astype(F32).astype(BF16)
    half = TILE // 2
    key_row = lax.broadcasted_iota(jnp.int32, (half, 2 * TILE), 0) + half
    block_info = []
    for b in range(2):
        west_block = pattern[2 * me + b, 0]
        east_block = pattern[2 * me + b, 2]
        picks = [(lax.rem(blk, 2) == 0) for blk in (west_block, east_block)]
        counts = (valid[west_block], own_count[b], valid[east_block])
        block_info.append((picks, counts))

    def heads_of(tensor):
        return jnp.concatenate((tensor * first, tensor * second), axis=0)

    def unfold(tensor):
        return jnp.concatenate(
            (tensor[: PAIR // 2, :TILE], tensor[PAIR // 2 :, TILE:]), axis=0
        ).T

    def step_pair(pair, carry):
        cols = columns(pair)

        @pl.when(pair + AHEAD < pairs)
        def _():
            send_halo(pair + AHEAD)

        for kind in range(2):
            for slot in range(2):
                halo_arrival(slot, kind, pair).wait_recv()

        edges = []
        far_total = [None, None]
        for b in range(2):
            picks, counts = block_info[b]
            band = pl.ds(b * TILE, TILE)
            sets = []
            for kind in range(2):
                near = []
                for slot in range(2):
                    near.append(
                        lax.select(
                            picks[slot],
                            halo[slot, kind, pl.ds(0, TILE), cols],
                            halo[slot, kind, pl.ds(TILE, TILE), cols],
                        )
                    )
                sets.append(
                    jnp.concatenate(
                        (near[0], kv_refs[kind][band, cols], near[1], far_kv[kind, :, cols]),
                        axis=0,
                    )
                )
            all_keys, all_values = sets
            query = heads_of(queries[band, cols] * jnp.asarray(0.125, BF16))
            grads = heads_of(grad_att[band, cols])
            scores = nt(all_keys, query)
            parts = []
            for slot in range(3):
                base = slot * TILE
                parts.append(scores[base : base + half])
                parts.append(
                    jnp.where(
                        key_row < counts[slot], scores[base + half : base + TILE], -jnp.inf
                    )
                )
            parts.append(scores[3 * TILE :])
            scores = jnp.concatenate(parts, axis=0)
            top = jnp.max(scores, axis=0, keepdims=True)
            weights = jnp.exp(scores - top)
            total = jnp.sum(weights, axis=0, keepdims=True)
            grad_chances = nt(all_values, grads)
            chances = weights * (1.0 / total)
            rounded = chances.astype(BF16)
            delta = jnp.sum(chances * grad_chances, axis=0, keepdims=True)
            grad_scores = (chances * (grad_chances - delta)).astype(BF16)
            attended[band, cols] = unfold(tn(all_values, rounded)).astype(BF16)
            grad_queries[band, cols] = (unfold(tn(all_keys, grad_scores)) * 0.125).astype(BF16)
            results = (nn(grad_scores, query), nn(rounded, grads))
            sides_of = []
            for kind in range(2):
                full = results[kind]
                own[kind, band, cols] = full[TILE : 2 * TILE]
                far = full[3 * TILE :]
                far_total[kind] = far if b == 0 else far_total[kind] + far
                sides_of.append((full[:TILE], full[2 * TILE : 3 * TILE]))
            edges.append(sides_of)

        for kind in range(2):
            far_sum[kind, :, cols] = far_total[kind].astype(BF16)
            for side in range(2):
                low = [jnp.where(block_info[b][0][side], 1.0, 0.0).astype(F32) for b in range(2)]
                one, two = edges[0][kind][side], edges[1][kind][side]
                back_out[side, kind, pl.ds(0, TILE), cols] = (
                    one * low[0] + two * low[1]
                ).astype(BF16)
                back_out[side, kind, pl.ds(TILE, TILE), cols] = (
                    one * (1.0 - low[0]) + two * (1.0 - low[1])
                ).astype(BF16)
        for kind in range(2):
            for side in range(2):
                back_copy(side, kind, pair).start()
        return carry

    lax.fori_loop(0, pairs, step_pair, 0)

    put_row = lax.broadcasted_iota(jnp.int32, (count * 16, n_blocks), 0)
    put_col = lax.broadcasted_iota(jnp.int32, (count * 16, n_blocks), 1)
    put_place = (put_col // 2) * 16 + put_col % 2
    packed = jnp.zeros((count * 16, GROUP), F32)
    for c in range(groups):
        for kind in range(2):
            chosen = (put_row == put_place + (4 * c + 2 * kind)).astype(F32).astype(BF16)
            packed += nn(chosen, far_sum[kind, :, c * GROUP : (c + 1) * GROUP])
    far_out[...] = packed.astype(BF16).reshape(count, 16, GROUP)
    far_in[me] = far_out[me]

    def send_far(step, carry):
        far_copy(step, peer(step), me).start()
        return carry

    lax.fori_loop(1, count, send_far, 0)

    for c in range(groups):
        part = slice(c * GROUP, (c + 1) * GROUP)
        layer_out[:, part] = nn(attended[...], weight[:, part]).astype(BF16)

    def take_far(step, carry):
        far_copy(step, peer(step), source(step)).wait_recv()
        return carry

    lax.fori_loop(1, count, take_far, 0)
    spread = jnp.sum(far_in[...].astype(F32), axis=0) / root
    live_row = lax.broadcasted_iota(jnp.int32, (TILE, GROUP), 0)
    outs = (grad_keys, grad_values)
    for c in range(groups):
        part = slice(c * GROUP, (c + 1) * GROUP)
        for pair in range(c * GROUP // PAIR, (c + 1) * GROUP // PAIR):
            for kind in range(2):
                for slot in range(2):
                    back_arrival(slot, kind, pair).wait_recv()
        for kind in range(2):
            for b in range(2):
                band = slice(b * TILE, (b + 1) * TILE)
                line = 4 * c + 2 * kind + b
                far = jnp.where(live_row < own_count[b], spread[line : line + 1, :], 0.0)
                outs[kind][band, part] = (
                    own[kind, band, part]
                    + back_in[0, kind, band, part].astype(F32)
                    + back_in[1, kind, band, part].astype(F32)
                    + far
                ).astype(BF16)

    def drain_pair(pair, carry):
        for kind in range(2):
            for side in range(2):
                halo_copy(side, kind, pair).wait_send()
                back_copy(side, kind, pair).wait_send()
        return carry

    lax.fori_loop(0, pairs, drain_pair, 0)

    def drain_peer(step, carry):
        summary_copy(step, me).wait_send()
        far_copy(step, peer(step), me).wait_send()
        return carry

    lax.fori_loop(1, count, drain_peer, 0)


def per_device(queries, key_tokens, value_tokens, grad_out, out_weight, pattern, valid_rows):
    count = lax.axis_size("lon")
    rows, features = queries.shape
    n_blocks = 2 * count
    pairs = features // PAIR
    shape = jax.ShapeDtypeStruct((rows, features), BF16)
    vmem = pl.BlockSpec(memory_space=pltpu.VMEM)
    smem = pl.BlockSpec(memory_space=pltpu.SMEM)
    dma = pltpu.SemaphoreType.DMA
    return pl.pallas_call(
        functools.partial(kernel, count),
        out_shape=(shape,) * 4,
        in_specs=[smem, smem] + [vmem] * 5,
        out_specs=(vmem,) * 4,
        scratch_shapes=[
            pltpu.VMEM((2, 2, rows, features), BF16),
            pltpu.VMEM((2, 2, rows, features), BF16),
            pltpu.VMEM((2, 2, rows, features), BF16),
            pltpu.VMEM((2, rows, features), F32),
            pltpu.VMEM((rows, features), BF16),
            pltpu.VMEM((rows, features), BF16),
            pltpu.VMEM((count, 16, GROUP), BF16),
            pltpu.VMEM((2, n_blocks, features), BF16),
            pltpu.VMEM((2, n_blocks, features), BF16),
            pltpu.VMEM((count, 16, GROUP), BF16),
            pltpu.VMEM((count, 16, GROUP), BF16),
            dma((2, 2, pairs)),
            dma((2, 2, pairs)),
            dma((2, 2, pairs)),
            dma((2, 2, pairs)),
            dma((count,)),
            dma((count,)),
            dma((count,)),
            dma((count,)),
        ],
        compiler_params=pltpu.CompilerParams(
            collective_id=0, has_side_effects=True, vmem_limit_bytes=48 * 2**20
        ),
        cost_estimate=pl.CostEstimate(
            flops=2_600_000_000, bytes_accessed=6_500_000, transcendentals=1_800_000
        ),
    )(pattern, valid_rows, queries, key_tokens, value_tokens, grad_out, out_weight)


def solution(mesh):
    split = P(("groups", "lon"), None)
    return jax.shard_map(
        per_device,
        mesh=mesh,
        in_specs=(split, split, split, split, P(), P(), P()),
        out_specs=(split,) * 4,
        check_vma=False,
    )
```

time: 215 us -> 71.1 us (0.33)
  local copies, waits for them, and re-layouts: 77.4 us -> 8.76 us
  Pallas kernels: 0 us -> 61.3 us
  matrix products: 38.8 us -> 0 us
  waiting for transfers between devices: 27.4 us -> 0 us
  blocking collectives: 25.8 us -> 0 us
  other arithmetic: 20.7 us -> 0 us
  between operations: 16.9 us -> 0.65 us
  starting transfers between devices: 6.92 us -> 0 us
    pallas_call x0 -> x1, Pallas kernels: none -> 61.3 us  [per_device(): pl.pallas_call(functools.partial(kernel, count), out_shape=(shape,) * 4,...]
    dot_general x16 -> x0, matrix products: 38.8 us -> none  [the longest x1 11.1 us: per_device(): jnp.einsum('ne,xnk->xek', onehot, stacked, precision=lax.Precision.HIGHEST)]
    unnamed x2 -> x0, waiting for transfers between devices: 27.4 us -> none
    another operation x11 -> x0, local copies, waits for them, and re-layouts: 26.6 us -> none  [the longest x2 13.3 us: per_device(): jnp.stack((near_grad_keys, near_grad_values))]
    all_gather x1 -> x0, blocking collectives: 25.8 us -> none  [per_device(): summaries = lax.all_gather(summary, 'lon', axis=1, tiled=True)]
    slice x5 -> x0, local copies, waits for them, and re-layouts: 13.3 us -> none  [the longest x2 7.98 us: per_device(): near_values = split_heads(near_pairs[1])]
    transpose x4 -> x0, local copies, waits for them, and re-layouts: 12.5 us -> none  [the longest x1 6.11 us: per_device(): jnp.einsum('bhtl,bthc->blhc', near_grad_scores, query_heads, preferred_el...]
    another operation x5 -> x0, other arithmetic: 10.1 us -> none
  transfers between devices with their start and end apart: 5 -> 0, of which waited for: 1 -> 0; matrix products, arithmetic and copies ran while one was open for 36% -> 0% of each run, Pallas kernels for 0% -> 0%
where the time goes in v1:
time: 71.1 us; the launch traced here: 70.7 us
  Pallas kernels  61.3 us (86%)
  local copies, waits for them, and re-layouts  8.76 us (12%)
    pallas_call x1, Pallas kernels, per_device(): pl.pallas_call(functools.partial(kernel, count), out_shape=(shape,) * 4,...  61.3 us
    unnamed x15, local copies, waits for them, and re-layouts  8.76 us

profile of v1, /device:TPU:0, one launch (start us, length us, event | category | flops | bytes accessed | tf_op | source)
XLA Modules:
  0.0 70.7 jit_solution(18438711590370640418)
XLA Ops:
  0.6 0.8 %copy.11.pattern = s32[32,3]{1,0:T(8,128)S(1)} copy(s32[32,3]{0,1:T(4,128)} %param.12) | data formatting | bytes 768 | tf_op args[5]
  1.4 0.0 copy-start
  1.4 1.0 %copy-done = bf16[256,1024]{1,0:T(8,128)(2,1)S(1)} copy-done((bf16[256,1024]{1,0:T(8,128)(2,1)S(1)}, bf16[256,1024]{1,0:T(8,128)(2,1)}, u32[]{:S(2)}) %copy-start) | copy-done | bytes 524312
  2.4 0.0 copy-start.1
  2.4 1.0 %copy-done.1 = bf16[256,1024]{1,0:T(8,128)(2,1)S(1)} copy-done((bf16[256,1024]{1,0:T(8,128)(2,1)S(1)}, bf16[256,1024]{1,0:T(8,128)(2,1)}, u32[]{:S(2)}) %copy-start.1) | copy-done | bytes 524312
  3.5 0.0 copy-start.2
  3.5 1.0 %copy-done.2 = bf16[256,1024]{1,0:T(8,128)(2,1)S(1)} copy-done((bf16[256,1024]{1,0:T(8,128)(2,1)S(1)}, bf16[256,1024]{1,0:T(8,128)(2,1)}, u32[]{:S(2)}) %copy-start.2) | copy-done | bytes 524312
  4.5 0.0 copy-start.3
  4.5 1.0 %copy-done.3 = bf16[256,1024]{1,0:T(8,128)(2,1)S(1)} copy-done((bf16[256,1024]{1,0:T(8,128)(2,1)S(1)}, bf16[256,1024]{1,0:T(8,128)(2,1)}, u32[]{:S(2)}) %copy-start.3) | copy-done | bytes 524312
  5.6 0.0 copy-start.4
  5.6 0.7 copy-done.4
  6.2 61.3 %shard_map.102 = (bf16[256,1024]{1,0:T(8,128)(2,1)S(1)}, bf16[256,1024]{1,0:T(8,128)(2,1)S(1)}, bf16[256,1024]{1,0:T(8,128)(2,1)S(1)}, bf16[256,1024]{1,0:T(8,128)(2,1)S(1)}) custom-call(s32[32,3]{1,0:T(8,128)S(1)} %copy.11.pattern, s32[32]{0:T(128)S(1)} %copy-done.4, bf16[256,1024]{1,0:T(8,128)(2,1)S(1)} %copy-done, bf16[256,1024]{1,0:T(8,128)(2,1)S(1)} %copy-done.1, ...), custom_call_target="tpu_custom_call" | custom-call | flops 2600000000 | bytes 6500000 | tf_op jit(solution)/shard_map/pallas_call | solution.py:361
  67.6 0.8 %copy.16 = bf16[256,1024]{1,0:T(8,128)(2,1)} copy(bf16[256,1024]{1,0:T(8,128)(2,1)S(1)} %get-tuple-element.8) | data formatting | bytes 1048576
  68.3 0.8 %copy.17 = bf16[256,1024]{1,0:T(8,128)(2,1)} copy(bf16[256,1024]{1,0:T(8,128)(2,1)S(1)} %get-tuple-element.9) | data formatting | bytes 1048576
  69.1 0.8 %copy.18 = bf16[256,1024]{1,0:T(8,128)(2,1)} copy(bf16[256,1024]{1,0:T(8,128)(2,1)S(1)} %get-tuple-element.10) | data formatting | bytes 1048576
  69.9 0.8 %copy.19 = bf16[256,1024]{1,0:T(8,128)(2,1)} copy(bf16[256,1024]{1,0:T(8,128)(2,1)S(1)} %get-tuple-element.11) | data formatting | bytes 1048576
Async XLA Ops:
  1.4 1.0 %copy-start = (bf16[256,1024]{1,0:T(8,128)(2,1)S(1)}, bf16[256,1024]{1,0:T(8,128)(2,1)}, u32[]{:S(2)}) copy-start(bf16[256,1024]{1,0:T(8,128)(2,1)} %queries.1) | copy-start | bytes 1572868
  2.4 1.0 %copy-start.1 = (bf16[256,1024]{1,0:T(8,128)(2,1)S(1)}, bf16[256,1024]{1,0:T(8,128)(2,1)}, u32[]{:S(2)}) copy-start(bf16[256,1024]{1,0:T(8,128)(2,1)} %keys.1) | copy-start | bytes 1572868
  3.5 1.0 %copy-start.2 = (bf16[256,1024]{1,0:T(8,128)(2,1)S(1)}, bf16[256,1024]{1,0:T(8,128)(2,1)}, u32[]{:S(2)}) copy-start(bf16[256,1024]{1,0:T(8,128)(2,1)} %values.1) | copy-start | bytes 1572868
  4.5 1.0 %copy-start.3 = (bf16[256,1024]{1,0:T(8,128)(2,1)S(1)}, bf16[256,1024]{1,0:T(8,128)(2,1)}, u32[]{:S(2)}) copy-start(bf16[256,1024]{1,0:T(8,128)(2,1)} %grad_out.1) | copy-start | bytes 1572868
  5.6 0.7 copy-start.4

commit v2 on v1

--- a/solution.py
+++ b/solution.py
@@ -11,7 +11,8 @@
 TILE = 128
 PAIR = 128
 GROUP = 256
-AHEAD = 2
+BEFORE = 1
+AHEAD = 4
 F32 = jnp.float32
 BF16 = jnp.bfloat16
 
@@ -30,8 +31,10 @@
 
 def kernel(
     count,
-    pattern, valid, queries, keys, values, grad_out, weight,
-    layer_out, grad_queries, grad_keys, grad_values,
+    pattern, valid, queries_hbm, keys_hbm, values_hbm, grad_out_hbm, weight_hbm,
+    layer_out_hbm, grad_queries_hbm, grad_keys_hbm, grad_values_hbm,
+    queries, keys, values, grad_out, weight,
+    layer_out, grad_queries, grad_keys, grad_values, load_sem, store_sem,
     halo, back_out, back_in, own, attended, grad_att,
     gathered, far_kv, far_sum, far_out, far_in,
     halo_send, halo_recv, back_send, back_recv,
@@ -62,7 +65,22 @@
         return carry
 
     lax.fori_loop(1, count, greet, 0)
-    pl.semaphore_wait(barrier, count - 1)
+    loads = [
+        pltpu.make_async_copy(far, near, load_sem.at[i])
+        for i, (far, near) in enumerate(
+            (
+                (keys_hbm, keys),
+                (values_hbm, values),
+                (grad_out_hbm, grad_out),
+                (weight_hbm, weight),
+                (queries_hbm, queries),
+            )
+        )
+    ]
+    for load in loads:
+        load.start()
+    loads[0].wait()
+    loads[1].wait()
 
     def columns(pair):
         return pl.ds(pl.multiple_of(pair * PAIR, PAIR), PAIR)
@@ -131,8 +149,6 @@
         for kind in range(2):
             for side in range(2):
                 halo_copy(side, kind, pair).start()
-
-    send_halo(0)
 
     own_count = [valid[2 * me + b] for b in range(2)]
     root_row = lax.broadcasted_iota(jnp.int32, (16, GROUP), 0)
@@ -156,19 +172,26 @@
         summary_copy(step, me).start()
         return carry
 
+    pl.semaphore_wait(barrier, count - 1)
     lax.fori_loop(1, count, send_summary, 0)
-    for pair in range(1, AHEAD):
+    for pair in range(BEFORE):
         send_halo(pair)
 
-    for c in range(groups):
+    for load in loads[2:]:
+        load.wait()
+    part = slice(0, GROUP)
+    grad_att[:, part] = nt(grad_out[...], weight[part, :]).astype(BF16)
+
+    def take_summary(step, carry):
+        summary_copy(step, source(step)).wait_recv()
+        return carry
+
+    lax.fori_loop(1, count, take_summary, 0)
+    for pair in range(BEFORE, AHEAD):
+        send_halo(pair)
+    for c in range(1, groups):
         part = slice(c * GROUP, (c + 1) * GROUP)
         grad_att[:, part] = nt(grad_out[...], weight[part, :]).astype(BF16)
-
-    def take_summary(step, carry):
-        summary_copy(step, source(step)).wait_recv()
-        return carry
-
-    lax.fori_loop(1, count, take_summary, 0)
     pieces = gathered[...].reshape(count * 16, GROUP)
     sel_row = lax.broadcasted_iota(jnp.int32, (n_blocks, count * 16), 0)
     sel_col = lax.broadcasted_iota(jnp.int32, (n_blocks, count * 16), 1)
@@ -185,8 +208,8 @@
     key_row = lax.broadcasted_iota(jnp.int32, (half, 2 * TILE), 0) + half
     block_info = []
     for b in range(2):
-        west_block = pattern[2 * me + b, 0]
-        east_block = pattern[2 * me + b, 2]
+        west_block = pattern[0, 2 * me + b]
+        east_block = pattern[2, 2 * me + b]
         picks = [(lax.rem(blk, 2) == 0) for blk in (west_block, east_block)]
         counts = (valid[west_block], own_count[b], valid[east_block])
         block_info.append((picks, counts))
@@ -305,6 +328,12 @@
     for c in range(groups):
         part = slice(c * GROUP, (c + 1) * GROUP)
         layer_out[:, part] = nn(attended[...], weight[:, part]).astype(BF16)
+    stores = [
+        pltpu.make_async_copy(layer_out, layer_out_hbm, store_sem.at[0]),
+        pltpu.make_async_copy(grad_queries, grad_queries_hbm, store_sem.at[1]),
+    ]
+    for store in stores:
+        store.start()
 
     def take_far(step, carry):
         far_copy(step, peer(step), source(step)).wait_recv()
@@ -314,6 +343,7 @@
     spread = jnp.sum(far_in[...].astype(F32), axis=0) / root
     live_row = lax.broadcasted_iota(jnp.int32, (TILE, GROUP), 0)
     outs = (grad_keys, grad_values)
+    outs_hbm = (grad_keys_hbm, grad_values_hbm)
     for c in range(groups):
         part = slice(c * GROUP, (c + 1) * GROUP)
         for pair in range(c * GROUP // PAIR, (c + 1) * GROUP // PAIR):
@@ -331,6 +361,11 @@
                     + back_in[1, kind, band, part].astype(F32)
                     + far
                 ).astype(BF16)
+            store = pltpu.make_async_copy(
+                outs[kind].at[:, part], outs_hbm[kind].at[:, part], store_sem.at[2 + 2 * c + kind]
+            )
+            store.start()
+            stores.append(store)
 
     def drain_pair(pair, carry):
         for kind in range(2):
@@ -347,6 +382,19 @@
         return carry
 
     lax.fori_loop(1, count, drain_peer, 0)
+    for store in stores:
+        store.wait()
+
+
+def hand_over(*refs):
+    sources, targets, sems = refs[:4], refs[4:8], refs[8]
+    copies = [
+        pltpu.make_async_copy(sources[i], targets[i], sems.at[i]) for i in range(4)
+    ]
+    for copy in copies:
+        copy.start()
+    for copy in copies:
+        copy.wait()
 
 
 def per_device(queries, key_tokens, value_tokens, grad_out, out_weight, pattern, valid_rows):
@@ -355,15 +403,26 @@
     n_blocks = 2 * count
     pairs = features // PAIR
     shape = jax.ShapeDtypeStruct((rows, features), BF16)
-    vmem = pl.BlockSpec(memory_space=pltpu.VMEM)
+    hbm = pl.BlockSpec(memory_space=pltpu.HBM)
     smem = pl.BlockSpec(memory_space=pltpu.SMEM)
     dma = pltpu.SemaphoreType.DMA
-    return pl.pallas_call(
+    outs = pl.pallas_call(
         functools.partial(kernel, count),
         out_shape=(shape,) * 4,
-        in_specs=[smem, smem] + [vmem] * 5,
-        out_specs=(vmem,) * 4,
+        in_specs=[smem, smem] + [hbm] * 5,
+        out_specs=(hbm,) * 4,
         scratch_shapes=[
+            pltpu.VMEM((rows, features), BF16),
+            pltpu.VMEM((rows, features), BF16),
+            pltpu.VMEM((rows, features), BF16),
+            pltpu.VMEM((rows, features), BF16),
+            pltpu.VMEM((features, features), BF16),
+            pltpu.VMEM((rows, features), BF16),
+            pltpu.VMEM((rows, features), BF16),
+            pltpu.VMEM((rows, features), BF16),
+            pltpu.VMEM((rows, features), BF16),
+            dma((5,)),
+            dma((2 + 2 * (features // GROUP),)),
             pltpu.VMEM((2, 2, rows, features), BF16),
             pltpu.VMEM((2, 2, rows, features), BF16),
             pltpu.VMEM((2, 2, rows, features), BF16),
@@ -385,12 +444,19 @@
             dma((count,)),
         ],
         compiler_params=pltpu.CompilerParams(
-            collective_id=0, has_side_effects=True, vmem_limit_bytes=48 * 2**20
+            collective_id=0, has_side_effects=True, vmem_limit_bytes=63 * 2**20
         ),
         cost_estimate=pl.CostEstimate(
             flops=2_600_000_000, bytes_accessed=6_500_000, transcendentals=1_800_000
         ),
-    )(pattern, valid_rows, queries, key_tokens, value_tokens, grad_out, out_weight)
+    )(pattern.T, valid_rows, queries, key_tokens, value_tokens, grad_out, out_weight)
+    return pl.pallas_call(
+        hand_over,
+        out_shape=(shape,) * 4,
+        in_specs=[hbm] * 4,
+        out_specs=(hbm,) * 4,
+        scratch_shapes=[dma((4,))],
+    )(*outs)
 
 
 def solution(mesh):

time: 71.1 us -> 126 us (1.77)
  Pallas kernels: 61.3 us -> 125 us
  local copies, waits for them, and re-layouts: 8.76 us -> 0 us
    pallas_call x0 -> x1, Pallas kernels: none -> 64.7 us  [per_device(): pl.pallas_call(hand_over, out_shape=(shape,) * 4, in_specs=[hbm] * 4, out...]
    unnamed x15 -> x0, local copies, waits for them, and re-layouts: 8.76 us -> none
where the time goes in v2:
time: 126 us; the launch traced here: 125 us
  Pallas kernels  125 us (99%)
    pallas_call x1, Pallas kernels, per_device(): pl.pallas_call(hand_over, out_shape=(shape,) * 4, in_specs=[hbm] * 4, out...  64.7 us
    pallas_call x1, Pallas kernels, per_device(): pl.pallas_call(functools.partial(kernel, count), out_shape=(shape,) * 4,...  60.2 us

profile of v2, /device:TPU:0, one launch (start us, length us, event | category | flops | bytes accessed | tf_op | source)
XLA Modules:
  0.0 125.5 jit_solution(10005271758328075816)
XLA Ops:
  0.6 60.2 %shard_map.102 = (bf16[256,1024]{1,0:T(8,128)(2,1)}, bf16[256,1024]{1,0:T(8,128)(2,1)}, bf16[256,1024]{1,0:T(8,128)(2,1)}, bf16[256,1024]{1,0:T(8,128)(2,1)}) custom-call(s32[3,32]{1,0:T(4,128)} %bitcast.1, s32[32]{0:T(128)} %valid.1, bf16[256,1024]{1,0:T(8,128)(2,1)} %queries_hbm.1, bf16[256,1024]{1,0:T(8,128)(2,1)} %keys_hbm.1, ...), custom_call_target="tpu_custom_call" | custom-call | flops 2600000000 | bytes 6500000 | tf_op jit(solution)/shard_map/pallas_call | solution.py:409
  60.8 64.7 %shard_map.103 = (bf16[256,1024]{1,0:T(8,128)(2,1)}, bf16[256,1024]{1,0:T(8,128)(2,1)}, bf16[256,1024]{1,0:T(8,128)(2,1)}, bf16[256,1024]{1,0:T(8,128)(2,1)}) custom-call(bf16[256,1024]{1,0:T(8,128)(2,1)} %get-tuple-element.8.refs_0_, bf16[256,1024]{1,0:T(8,128)(2,1)} %get-tuple-element.9.refs_1_, bf16[256,1024]{1,0:T(8,128)(2,1)} %get-tuple-element.10.refs_2_, ...), custom_call_target="tpu_custom_call" | custom-call | tf_op jit(solution)/shard_map/pallas_call | solution.py:453

commit v3 on v2

--- a/solution.py
+++ b/solution.py
@@ -11,7 +11,7 @@
 TILE = 128
 PAIR = 128
 GROUP = 256
-BEFORE = 1
+BEFORE = 2
 AHEAD = 4
 F32 = jnp.float32
 BF16 = jnp.bfloat16
@@ -387,14 +387,16 @@
 
 
 def hand_over(*refs):
-    sources, targets, sems = refs[:4], refs[4:8], refs[8]
-    copies = [
-        pltpu.make_async_copy(sources[i], targets[i], sems.at[i]) for i in range(4)
-    ]
-    for copy in copies:
-        copy.start()
-    for copy in copies:
-        copy.wait()
+    sources, targets, buffers, load_sem, store_sem = refs[:4], refs[4:8], refs[8], refs[9], refs[10]
+    loads = [pltpu.make_async_copy(sources[i], buffers.at[i], load_sem.at[i]) for i in range(4)]
+    stores = [pltpu.make_async_copy(buffers.at[i], targets[i], store_sem.at[i]) for i in range(4)]
+    for load in loads:
+        load.start()
+    for load, store in zip(loads, stores):
+        load.wait()
+        store.start()
+    for store in stores:
+        store.wait()
 
 
 def per_device(queries, key_tokens, value_tokens, grad_out, out_weight, pattern, valid_rows):
@@ -455,7 +457,7 @@
         out_shape=(shape,) * 4,
         in_specs=[hbm] * 4,
         out_specs=(hbm,) * 4,
-        scratch_shapes=[dma((4,))],
+        scratch_shapes=[pltpu.VMEM((4, rows, features), BF16), dma((4,)), dma((4,))],
     )(*outs)
 
 

time: 126 us -> 62.4 us (0.50)
  Pallas kernels: 125 us -> 61.6 us
    pallas_call x1, Pallas kernels: 64.7 us -> 2.42 us  [per_device(): pl.pallas_call(hand_over, out_shape=(shape,) * 4, in_specs=[hbm] * 4, out...]
where the time goes in v3:
time: 62.4 us; the launch traced here: 62.2 us
  Pallas kernels  61.6 us (99%)
  between operations  0.64 us (1%)
    pallas_call x1, Pallas kernels, per_device(): pl.pallas_call(functools.partial(kernel, count), out_shape=(shape,) * 4,...  59.2 us
    pallas_call x1, Pallas kernels, per_device(): pl.pallas_call(hand_over, out_shape=(shape,) * 4, in_specs=[hbm] * 4, out...  2.42 us

profile of v3, /device:TPU:0, one launch (start us, length us, event | category | flops | bytes accessed | tf_op | source)
XLA Modules:
  0.0 62.2 jit_solution(765543328240871809)
XLA Ops:
  0.6 59.2 %shard_map.102 = (bf16[256,1024]{1,0:T(8,128)(2,1)}, bf16[256,1024]{1,0:T(8,128)(2,1)}, bf16[256,1024]{1,0:T(8,128)(2,1)}, bf16[256,1024]{1,0:T(8,128)(2,1)}) custom-call(s32[3,32]{1,0:T(4,128)} %bitcast.1, s32[32]{0:T(128)} %valid.1, bf16[256,1024]{1,0:T(8,128)(2,1)} %queries_hbm.1, bf16[256,1024]{1,0:T(8,128)(2,1)} %keys_hbm.1, ...), custom_call_target="tpu_custom_call" | custom-call | flops 2600000000 | bytes 6500000 | tf_op jit(solution)/shard_map/pallas_call | solution.py:411
  59.8 2.4 %shard_map.103 = (bf16[256,1024]{1,0:T(8,128)(2,1)}, bf16[256,1024]{1,0:T(8,128)(2,1)}, bf16[256,1024]{1,0:T(8,128)(2,1)}, bf16[256,1024]{1,0:T(8,128)(2,1)}) custom-call(bf16[256,1024]{1,0:T(8,128)(2,1)} %get-tuple-element.8.refs_0_, bf16[256,1024]{1,0:T(8,128)(2,1)} %get-tuple-element.9.refs_1_, bf16[256,1024]{1,0:T(8,128)(2,1)} %get-tuple-element.10.refs_2_, ...), custom_call_target="tpu_custom_call" | custom-call | tf_op jit(solution)/shard_map/pallas_call | solution.py:455

commit v4 on v3

--- a/solution.py
+++ b/solution.py
@@ -13,6 +13,7 @@
 GROUP = 256
 BEFORE = 2
 AHEAD = 4
+SPLIT = 4
 F32 = jnp.float32
 BF16 = jnp.bfloat16
 
@@ -388,8 +389,16 @@
 
 def hand_over(*refs):
     sources, targets, buffers, load_sem, store_sem = refs[:4], refs[4:8], refs[8], refs[9], refs[10]
-    loads = [pltpu.make_async_copy(sources[i], buffers.at[i], load_sem.at[i]) for i in range(4)]
-    stores = [pltpu.make_async_copy(buffers.at[i], targets[i], store_sem.at[i]) for i in range(4)]
+    size = buffers.shape[1] // SPLIT
+    loads, stores = [], []
+    for n in range(4 * SPLIT):
+        i, band = n // SPLIT, pl.ds(n % SPLIT * size, size)
+        loads.append(
+            pltpu.make_async_copy(sources[i].at[band], buffers.at[i, band], load_sem.at[n])
+        )
+        stores.append(
+            pltpu.make_async_copy(buffers.at[i, band], targets[i].at[band], store_sem.at[n])
+        )
     for load in loads:
         load.start()
     for load, store in zip(loads, stores):
@@ -457,7 +466,9 @@
         out_shape=(shape,) * 4,
         in_specs=[hbm] * 4,
         out_specs=(hbm,) * 4,
-        scratch_shapes=[pltpu.VMEM((4, rows, features), BF16), dma((4,)), dma((4,))],
+        scratch_shapes=[
+            pltpu.VMEM((4, rows, features), BF16), dma((4 * SPLIT,)), dma((4 * SPLIT,))
+        ],
     )(*outs)
 
 

time: 62.4 us -> 62.6 us (level)
  no operation moved by 1% of the time
where the time goes in v4:
time: 62.6 us; the launch traced here: 62.4 us
  Pallas kernels  61.7 us (99%)
  between operations  0.64 us (1%)
    pallas_call x1, Pallas kernels, per_device(): pl.pallas_call(functools.partial(kernel, count), out_shape=(shape,) * 4,...  59.2 us
    pallas_call x1, Pallas kernels, per_device(): pl.pallas_call(hand_over, out_shape=(shape,) * 4, in_specs=[hbm] * 4, out...  2.57 us

profile of v4, /device:TPU:0, one launch (start us, length us, event | category | flops | bytes accessed | tf_op | source)
XLA Modules:
  0.0 62.4 jit_solution(10222497292780365519)
XLA Ops:
  0.6 59.2 %shard_map.102 = (bf16[256,1024]{1,0:T(8,128)(2,1)}, bf16[256,1024]{1,0:T(8,128)(2,1)}, bf16[256,1024]{1,0:T(8,128)(2,1)}, bf16[256,1024]{1,0:T(8,128)(2,1)}) custom-call(s32[3,32]{1,0:T(4,128)} %bitcast.1, s32[32]{0:T(128)} %valid.1, bf16[256,1024]{1,0:T(8,128)(2,1)} %queries_hbm.1, bf16[256,1024]{1,0:T(8,128)(2,1)} %keys_hbm.1, ...), custom_call_target="tpu_custom_call" | custom-call | flops 2600000000 | bytes 6500000 | tf_op jit(solution)/shard_map/pallas_call | solution.py:420
  59.8 2.6 %shard_map.103 = (bf16[256,1024]{1,0:T(8,128)(2,1)}, bf16[256,1024]{1,0:T(8,128)(2,1)}, bf16[256,1024]{1,0:T(8,128)(2,1)}, bf16[256,1024]{1,0:T(8,128)(2,1)}) custom-call(bf16[256,1024]{1,0:T(8,128)(2,1)} %get-tuple-element.8.refs_0_, bf16[256,1024]{1,0:T(8,128)(2,1)} %get-tuple-element.9.refs_1_, bf16[256,1024]{1,0:T(8,128)(2,1)} %get-tuple-element.10.refs_2_, ...), custom_call_target="tpu_custom_call" | custom-call | tf_op jit(solution)/shard_map/pallas_call | solution.py:464
